TPU v7x, 32 devices: a whole 2x2x4 slice. The times are simulated.
32 devices in a mesh: rep: 2 (over y), gx: 4 (over z), gy: 4 (over x, core).
Axes of the slice: x: 2, y: 2, z: 4, core: 2. Of those that a mesh axis runs over, the one named last changes fastest.
Arguments:
- positions: float32 [8, 4, 3, 128], P(('rep', 'gx'), 'gy'), parts along dimension 0, as said below
- species: int32 [8, 4, 128], P(('rep', 'gx'), 'gy'), parts along dimension 0, may hold values from 0 to 5
- neighbours: int32 [8, 4, 8, 128], P(('rep', 'gx'), 'gy'), parts along dimension 0, may hold values from 0 to 287, as said below
- neighbour_count: int32 [8, 4, 128], P(('rep', 'gx'), 'gy'), parts along dimension 0, may hold values from 4 to 8
- face_rows: int32 [8, 4, 4, 32], P(('rep', 'gx'), 'gy'), parts along dimension 0, may hold values from 0 to 127, as said below
- corner_rows: int32 [8, 4, 4, 8], P(('rep', 'gx'), 'gy'), parts along dimension 0, may hold values from 0 to 127, as said below
- species_embed: float32 [6, 128], replicated, may hold values from -5 to 5
- atom_energy: float32 [6], replicated, may hold values from -4 to 4
- radial_in: float32 [2, 8, 64], replicated, may hold values from -4 to 4
- radial_out: float32 [2, 64, 512], replicated, may hold values from -1.5 to 1.5
- mixing: float32 [2, 3, 128, 128], replicated, may hold values from -0.5 to 0.5
- vector_mix: float32 [128, 128], replicated, may hold values from -0.5 to 0.5
- readout: float32 [2, 128], replicated, may hold values from -0.5 to 0.5
Outputs:
- node_energy: float32 [8, 4, 128], P(('rep', 'gx'), 'gy'), parts along dimension 0
- forces: float32 [8, 4, 3, 128], P(('rep', 'gx'), 'gy'), parts along dimension 0
There are 2 independent parts, one for each index of `rep`. A program takes and returns all parts, laid end to end along the dimension named above; an argument that names none is the same for every part. Nothing has to cross between parts.
Inputs may be any that keep to these rules, and one draw needn't show every extreme that they name: `positions`: coordinates x and y lie in 0 to 17.6, z in 0 to 2.2 * 2; the atoms of one column's table, with the offsets added, are at least 0.5 apart. `neighbours`: the 8 slots of one atom name distinct rows of its column's table, never the atom itself. face_rows[x, y, f] holds 32 distinct atoms of column (x, y); they become face block f of the column at (x, y) minus the f-th face offset. corner_rows[x, y, c] holds 8 distinct atoms of column (x, y); they become corner block c of the column at (x, y) minus the c-th corner offset.
All inputs are finite; a program needn't handle non-finite values.
Results may differ from a plain program's by a relative error of at most 0.0003.
Values sent between devices are 32-bit elements; how exact they have to be, the bound alone decides.
A program may use at most 128 MiB of HBM per device.

v0:
```python
import math

import jax
import jax.numpy as jnp
from jax import lax
from jax.experimental import pallas as pl
from jax.experimental.pallas import tpu as pltpu
from jax.sharding import PartitionSpec as P

cutoff = 5.0
column_width = 17.6
face_offsets = ((-1, 0), (1, 0), (0, -1), (0, 1))
corner_offsets = ((-1, -1), (1, -1), (-1, 1), (1, 1))
offsets = face_offsets + corner_offsets
f32 = jnp.float32
bf16 = jnp.bfloat16
MESH = pl.DeviceIdType.MESH
lane = 128
block = 32

sin_terms = [(-1) ** m * math.pi ** (2 * m + 1) / math.factorial(2 * m + 1) for m in range(8)]
cos_terms = [(-1) ** m * math.pi ** (2 * m) / math.factorial(2 * m) for m in range(8)]


def horner(terms, z):
    total = jnp.full_like(z, terms[-1])
    for term in terms[-2::-1]:
        total = total * z + term
    return total


def split(x):
    high = x.astype(bf16)
    return high, (x - high.astype(f32)).astype(bf16)


def thirds(x):
    high = x.astype(bf16).astype(f32)
    rest = x - high
    middle = rest.astype(bf16).astype(f32)
    return high, middle, rest - middle


def dot(a, b):
    return lax.dot_general(a, b, (((1,), (0,)), ((), ())), preferred_element_type=f32)


def dot_nt(a, b):
    return lax.dot_general(a, b, (((1,), (1,)), ((), ())), preferred_element_type=f32)


def dot3(a, b):
    return dot(a[0], b[0]) + (dot(a[0], b[1]) + dot(a[1], b[0]))


def fold(x):
    total = x[0:8]
    for start in range(8, x.shape[0], 8):
        total = total + x[start : start + 8]
    return total


def kernel(
    sizes,
    positions, species, neighbours, counts, faces, corners, embed, atom_energy,
    radial_in, radial_out, mixing, vector_mix, readout,
    energy_out, force_out,
    small, gather, picks, picks_t, mix, mix_t, rad_t, rad, w1, w2, h1, h2, unit,
    message, grad_message, dw_high, dw_low, dh_high, dh_low, du, tangent, hidden,
    state, start, layer, features, back,
    out0, in0, out1, in1, out2, in2, out3, in3, send_sem, recv_sem,
):
    count_x, count_y = sizes
    me_x, me_y = lax.axis_index("gx"), lax.axis_index("gy")
    atoms = positions.shape[3]
    slots = neighbours.shape[2]
    edges = slots * atoms
    kinds, channels = embed.shape
    orders, width = radial_in.shape[1:]
    face_width, corner_width = faces.shape[3], corners.shape[3]
    spans = []
    cursor = 0
    for offset in offsets:
        rows = face_width if offset in face_offsets else corner_width
        spans.append((cursor, rows))
        cursor += rows
    ghosts = cursor
    padded = 2 * lane

    def place(offset, sign):
        return {
            "gx": lax.rem(me_x + sign * offset[0] + count_x, count_x),
            "gy": lax.rem(me_y + sign * offset[1] + count_y, count_y),
        }

    barrier = pltpu.get_barrier_semaphore()
    for offset in offsets:
        pl.semaphore_signal(barrier, inc=1, device_id=place(offset, 1), device_id_type=MESH)

    def exchange(phase, source, target, sign):
        copies = []
        for which, offset in enumerate(offsets):
            first, rows = spans[which]
            copies.append(
                pltpu.make_async_remote_copy(
                    src_ref=source.at[pl.ds(first, rows)],
                    dst_ref=target.at[pl.ds(first, rows)],
                    send_sem=send_sem.at[phase, which],
                    recv_sem=recv_sem.at[phase, which],
                    device_id=place(offset, sign),
                    device_id_type=MESH,
                )
            )
        for copy in copies[4:] + copies[:4]:
            copy.start()
        return copies

    def arrive(copies):
        for copy in copies:
            copy.wait_recv()

    def pad_rows(x, rows):
        return jnp.concatenate([x, jnp.zeros((rows - x.shape[0], x.shape[1]), x.dtype)], axis=0)

    chosen = jnp.concatenate(
        [faces[0, 0, f : f + 1, :] for f in range(4)]
        + [corners[0, 0, c : c + 1, :] for c in range(4)]
        + [jnp.full((1, padded - ghosts), -1, jnp.int32)],
        axis=1,
    )
    onehot = (lax.broadcasted_iota(jnp.int32, (atoms, padded), 0) == chosen).astype(f32)
    picks_t[...] = onehot.astype(bf16)
    picks[...] = onehot.T[:ghosts].astype(bf16)

    code = species[0].astype(f32)
    small[...] = jnp.zeros_like(small)
    small[0:3, :] = positions[0, 0]
    small[3:4, :] = code
    own = small[0:8, :]
    own_parts = thirds(own)
    packet = 0.0
    for part in own_parts:
        packet = packet + dot_nt(picks[...], pad_rows(part, lane).astype(bf16))
    row = lax.broadcasted_iota(jnp.int32, (ghosts, lane), 0)
    column = lax.broadcasted_iota(jnp.int32, (ghosts, lane), 1)
    shift_x = jnp.zeros((ghosts, lane), f32)
    shift_y = jnp.zeros((ghosts, lane), f32)
    for which, offset in enumerate(offsets):
        first, rows = spans[which]
        inside = (row >= first) & (row < first + rows)
        shift_x = jnp.where(inside, offset[0] * column_width, shift_x)
        shift_y = jnp.where(inside, offset[1] * column_width, shift_y)
    out0[...] = packet + jnp.where(column == 0, shift_x, jnp.where(column == 1, shift_y, 0.0))
    pl.semaphore_wait(barrier, len(offsets))
    sent0 = exchange(0, out0, in0, -1)

    for k in range(slots):
        lanes = slice(k * lane, (k + 1) * lane)
        where = neighbours[0, 0, k : k + 1, :]
        hit = lax.broadcasted_iota(jnp.int32, (atoms + ghosts, lane), 0) == where
        gather[:, lanes] = hit.astype(f32).astype(bf16)
    local_pick = gather[0:atoms, :]
    ghost_pick = gather[atoms : atoms + ghosts, :]

    own_stack = pad_rows(jnp.concatenate(own_parts, axis=0), 32).astype(bf16)
    near = dot(own_stack, gather[0:atoms, :])

    for m in range(7):
        matrix = vector_mix[...] if m == 6 else mixing[m // 3, m % 3]
        mix[0, m], mix[1, m] = split(matrix)
        mix_t[0, m], mix_t[1, m] = split(matrix.T)

    def forward(m, x):
        parts = split(x)
        return dot3((mix_t[0, m], mix_t[1, m]), parts)

    def backward(m, x):
        parts = split(x)
        return dot3((mix[0, m], mix[1, m]), parts)

    both = jnp.concatenate([radial_out[0], radial_out[1]], axis=0)
    rad[0:128, :], rad[128:256, :] = split(both)
    turned = both.T
    turned_high = turned.astype(bf16).astype(f32)
    turned_low = turned - turned_high
    for l in range(2):
        c = slice(l * width, (l + 1) * width)
        rad_t[l] = jnp.concatenate(
            [turned_high[:, c], turned_high[:, c], turned_low[:, c]], axis=1
        ).astype(bf16)

    first_in = jnp.concatenate([radial_in[0], radial_in[1]], axis=1)
    first_high, first_middle, unused = thirds(first_in)
    first_mat = pad_rows(
        jnp.concatenate([first_high, first_high, first_middle], axis=0), lane
    ).T[:, :32].astype(bf16)

    small[8 : 8 + kinds, :] = embed[...]
    embed_mat = pad_rows(jnp.concatenate(thirds(small[8:16, :]), axis=0), lane).T[:, :32].astype(bf16)
    row8 = lax.broadcasted_iota(jnp.int32, (8, edges), 0)
    row8f = row8.astype(f32)

    def species_features(codes):
        hits = (row8f[:, : codes.shape[1]] == codes).astype(f32)
        return dot(embed_mat, pad_rows(jnp.concatenate([hits, hits, hits], axis=0), 32).astype(bf16))

    start[...] = species_features(code)
    readout_first = jnp.broadcast_to(readout[0:1, :], (lane, lane)).T
    readout_second = jnp.broadcast_to(readout[1:2, :], (lane, lane)).T
    pull_second = backward(5, readout_second)
    live = jnp.concatenate(
        [jnp.where(counts[0] > k, 1.0 / math.sqrt(slots), 0.0) for k in range(slots)], axis=1
    )
    centre = jnp.where(row8[:, :atoms] < 3, own, 0.0)
    centre = jnp.concatenate([centre] * slots, axis=1)

    arrive(sent0)
    arrived = pad_rows(in0[...], padded).T[0:8, :ghosts]
    arrived = pad_rows(jnp.concatenate(thirds(arrived), axis=0), 32).astype(bf16)
    far = dot(arrived, gather[atoms : atoms + ghosts, :])
    table = near + far
    table = (table[0:8] + table[8:16]) + table[16:24]
    codes = table[3:4, :]
    relative = jnp.where(row8 < 3, table - centre, 0.0)
    distance = jnp.sqrt(jnp.sum(relative * relative, axis=0, keepdims=True))
    inverse = 1.0 / distance
    direction = relative * inverse
    unit[...] = direction
    s = jnp.minimum(distance * (1.0 / cutoff), 1.0)
    s2 = s * s
    s5 = s2 * s2 * s
    envelope = 1.0 + s5 * s * (-28.0 + s * (48.0 - 21.0 * s))
    scale = envelope * live
    scale_slope = (-168.0 / cutoff) * s5 * (1.0 - s) * (1.0 - s) * live
    harmonic = row8f + 1.0
    turns = harmonic * s
    nearest = jnp.floor(turns + 0.5)
    y = turns - nearest
    half = nearest * 0.5
    sign = 1.0 - 4.0 * (half - jnp.floor(half))
    z = y * y
    sine = sign * y * horner(sin_terms, z)
    cosine = sign * horner(cos_terms, z)
    norm = math.sqrt(2.0 / cutoff) * inverse
    bessel = norm * sine
    bessel_slope = norm * ((math.pi / cutoff) * harmonic * cosine - sine * inverse)

    def hidden_input(x):
        high = x.astype(bf16).astype(f32)
        low = x - high
        stack = pad_rows(jnp.concatenate([high, low, high], axis=0), 32).astype(bf16)
        return dot(first_mat, stack)

    pre = hidden_input(bessel)
    pre_slope = hidden_input(bessel_slope)
    gate = 1.0 / (1.0 + jnp.exp(-pre))
    silu = pre * gate
    slope = gate * (1.0 + pre * (1.0 - gate))
    tangent[...] = scale_slope * silu + scale * slope * pre_slope
    scaled = scale * silu
    scaled_high, scaled_low = split(scaled)
    hidden[0] = jnp.concatenate(
        [scaled_high[:width], scaled_low[:width], scaled_high[:width]], axis=0
    )
    hidden[1] = jnp.concatenate(
        [scaled_high[width:], scaled_low[width:], scaled_high[width:]], axis=0
    )
    c1, c2, c3, c4 = channels, 2 * channels, 3 * channels, 4 * channels
    w1[0:c1, :] = dot(rad_t[0, 0:c1, :], hidden[0])
    w1[c1:c2, :] = dot(rad_t[0, c2:c3, :], hidden[0])
    h1[...] = species_features(codes)

    blocks = channels // block

    def units(lanes):
        return [unit[m : m + 1, lanes] for m in range(3)]

    def first_messages(step, carry):
        c = pl.multiple_of(step * block, block)
        total = [jnp.zeros((block, lane), f32) for m in range(4)]
        for k in range(slots):
            lanes = slice(k * lane, (k + 1) * lane)
            u = units(lanes)
            source = h1[pl.ds(c, block), lanes]
            total[0] = total[0] + w1[pl.ds(c, block), lanes] * source
            across = w1[pl.ds(c1 + c, block), lanes] * source
            for m in range(3):
                total[1 + m] = total[1 + m] + u[m] * across
        for m in range(4):
            message[pl.ds(m * c1 + c, block), :] = total[m]
        return carry

    lax.fori_loop(0, blocks, first_messages, 0)

    def side_by_side(x):
        return jnp.concatenate([x[c1:c2], x[c2:c3], x[c3:c4]], axis=1)

    def parts3(x):
        return x[:, 0:lane], x[:, lane : 2 * lane], x[:, 2 * lane : 3 * lane]

    scalar = forward(0, message[0:c1, :])
    vector = forward(1, side_by_side(message[...]))
    vx, vy, vz = parts3(vector)
    square = scalar * scalar + (vx * vx + vy * vy + vz * vz)
    scalar3 = jnp.concatenate([scalar, scalar, scalar], axis=1)
    new_scalar = start[...] + scalar + forward(2, square)
    new_vector = vector + forward(6, scalar3 * vector)
    state[:, 0:lane] = scalar
    state[:, lane : 4 * lane] = vector
    layer[0:c1, :] = new_scalar
    nx, ny, nz = parts3(new_vector)
    layer[c1:c2, :] = nx
    layer[c2:c3, :] = ny
    layer[c3:c4, :] = nz

    layer_high, layer_low = split(layer[...])
    features[:, 0:lane] = layer_high
    features[:, lane : 2 * lane] = layer_low
    out1[...] = dot_nt(picks[...], layer_high) + dot_nt(picks[...], layer_low)
    sent1 = exchange(1, out1, in1, -1)

    w2[...] = dot(rad_t[1], hidden[1])
    h2[...] = dot(
        features[...], jnp.concatenate([gather[0:atoms, :], gather[0:atoms, :]], axis=0)
    )
    arrive(sent1)
    far_features = pad_rows(in1[...], padded).T[:, :ghosts]
    far_high, far_low = split(far_features)
    h2[...] += dot(far_high, gather[atoms : atoms + ghosts, :]) + dot(
        far_low, gather[atoms : atoms + ghosts, :]
    )

    def second_messages(step, carry):
        c = pl.multiple_of(step * block, block)
        total = [jnp.zeros((block, lane), f32) for m in range(4)]
        for k in range(slots):
            lanes = slice(k * lane, (k + 1) * lane)
            u = units(lanes)
            w = [w2[pl.ds(m * c1 + c, block), lanes] for m in range(4)]
            h = [h2[pl.ds(m * c1 + c, block), lanes] for m in range(4)]
            along = u[0] * h[1] + u[1] * h[2] + u[2] * h[3]
            total[0] = total[0] + (w[0] * h[0] + w[1] * along)
            across = w[2] * h[0]
            for m in range(3):
                total[1 + m] = total[1 + m] + (u[m] * across + w[3] * h[1 + m])
        for m in range(4):
            message[pl.ds(m * c1 + c, block), :] = total[m]
        return carry

    lax.fori_loop(0, blocks, second_messages, 0)
    scalar2 = forward(3, message[0:c1, :])
    vector2 = forward(4, side_by_side(message[...]))
    grad_scalar2 = readout_second + 2.0 * scalar2 * pull_second
    grad_vector2 = 2.0 * vector2 * jnp.concatenate([pull_second] * 3, axis=1)

    def store_grad(first, second):
        grad_message[0:c1, :] = first
        sx, sy, sz = parts3(second)
        grad_message[c1:c2, :] = sx
        grad_message[c2:c3, :] = sy
        grad_message[c3:c4, :] = sz

    store_grad(backward(3, grad_scalar2), backward(4, grad_vector2))
    du[...] = jnp.zeros_like(du)

    def store_split(high, low, at, lanes, x):
        a, b = split(x)
        high[pl.ds(at, block), lanes] = a
        low[pl.ds(at, block), lanes] = b

    def second_grads(step, carry):
        c = pl.multiple_of(step * block, block)
        d = [grad_message[pl.ds(m * c1 + c, block), :] for m in range(4)]
        for k in range(slots):
            lanes = slice(k * lane, (k + 1) * lane)
            u = units(lanes)
            w = [w2[pl.ds(m * c1 + c, block), lanes] for m in range(4)]
            h = [h2[pl.ds(m * c1 + c, block), lanes] for m in range(4)]
            along = u[0] * h[1] + u[1] * h[2] + u[2] * h[3]
            turn = u[0] * d[1] + u[1] * d[2] + u[2] * d[3]
            store_split(dw_high, dw_low, c, lanes, d[0] * h[0])
            store_split(dw_high, dw_low, c1 + c, lanes, d[0] * along)
            store_split(dw_high, dw_low, c2 + c, lanes, turn * h[0])
            store_split(
                dw_high, dw_low, c3 + c, lanes, d[1] * h[1] + d[2] * h[2] + d[3] * h[3]
            )
            store_split(dh_high, dh_low, c, lanes, w[0] * d[0] + w[2] * turn)
            inward = w[1] * d[0]
            across = w[2] * h[0]
            for m in range(3):
                store_split(
                    dh_high, dh_low, (1 + m) * c1 + c, lanes, inward * u[m] + w[3] * d[1 + m]
                )
                du[m * 8 : m * 8 + 8, lanes] += fold(inward * h[1 + m] + across * d[1 + m])
        return carry

    lax.fori_loop(0, blocks, second_grads, 0)
    out2[...] = dot_nt(gather[atoms : atoms + ghosts, :], dh_high[...]) + dot_nt(
        gather[atoms : atoms + ghosts, :], dh_low[...]
    )
    sent2 = exchange(2, out2, in2, 1)

    back[...] = dot_nt(gather[0:atoms, :], dh_high[...]) + dot_nt(gather[0:atoms, :], dh_low[...])
    hidden_rows = slice(width, 2 * width)
    pulled = dot(rad[width : 2 * width, :], dw_high[...])
    pulled = pulled + dot(rad[width : 2 * width, :], dw_low[...])
    pulled = pulled + dot(rad[128 + width : 128 + 2 * width, :], dw_high[...])
    radial_grad = jnp.sum(pulled * tangent[hidden_rows, :], axis=0, keepdims=True)

    square2 = scalar2 * scalar2 + sum(p * p for p in parts3(vector2))
    final = layer[0:c1, :] + scalar2 + forward(5, square2)
    energy = jnp.sum(readout_first * layer[0:c1, :] + readout_second * final, axis=0, keepdims=True)
    for kind in range(kinds):
        energy = energy + jnp.where(code == float(kind), atom_energy[kind], 0.0)
    energy_out[0] = energy

    arrive(sent2)
    in2_high, in2_low = split(in2[...])
    picked = picks_t[:, :ghosts]
    total_back = back[...] + (dot(picked, in2_high) + dot(picked, in2_low))
    grad_state = total_back.T
    g0 = grad_state[0:c1] + (readout_first + readout_second)
    g1 = side_by_side(grad_state)
    scalar = state[:, 0:lane]
    vector = state[:, lane : 4 * lane]
    pull = backward(2, g0)
    cross = backward(6, g1)
    crossed = parts3(cross * vector)
    grad_scalar = g0 + 2.0 * scalar * pull + (crossed[0] + crossed[1] + crossed[2])
    grad_vector = (
        g1
        + 2.0 * vector * jnp.concatenate([pull] * 3, axis=1)
        + jnp.concatenate([scalar] * 3, axis=1) * cross
    )
    store_grad(backward(0, grad_scalar), backward(1, grad_vector))

    def first_grads(step, carry):
        c = pl.multiple_of(step * block, block)
        d = [grad_message[pl.ds(m * c1 + c, block), :] for m in range(4)]
        for k in range(slots):
            lanes = slice(k * lane, (k + 1) * lane)
            u = units(lanes)
            source = h1[pl.ds(c, block), lanes]
            turn = u[0] * d[1] + u[1] * d[2] + u[2] * d[3]
            store_split(dw_high, dw_low, c, lanes, d[0] * source)
            store_split(dw_high, dw_low, c1 + c, lanes, turn * source)
            across = w1[pl.ds(c1 + c, block), lanes] * source
            for m in range(3):
                du[m * 8 : m * 8 + 8, lanes] += fold(across * d[1 + m])
        return carry

    lax.fori_loop(0, blocks, first_grads, 0)
    rad_high = jnp.concatenate([rad[0:width, 0:c1], rad[0:width, c2:c3]], axis=1)
    rad_low = jnp.concatenate([rad[128 : 128 + width, 0:c1], rad[128 : 128 + width, c2:c3]], axis=1)
    pulled = dot(rad_high, dw_high[0:c2, :]) + dot(rad_high, dw_low[0:c2, :])
    pulled = pulled + dot(rad_low, dw_high[0:c2, :])
    radial_grad = radial_grad + jnp.sum(pulled * tangent[0:width, :], axis=0, keepdims=True)

    turn_grad = jnp.concatenate(
        [jnp.sum(du[m * 8 : m * 8 + 8, :], axis=0, keepdims=True) for m in range(3)]
        + [jnp.zeros((5, edges), f32)],
        axis=0,
    )
    direction = unit[...]
    outward = jnp.sum(direction * turn_grad, axis=0, keepdims=True)
    pair = (turn_grad - direction * outward) * inverse + direction * radial_grad
    pair_high, pair_low = split(pad_rows(pair, lane))
    out3[...] = dot_nt(gather[atoms : atoms + ghosts, :], pair_high) + dot_nt(
        gather[atoms : atoms + ghosts, :], pair_low
    )
    sent3 = exchange(3, out3, in3, 1)
    mine = dot_nt(gather[0:atoms, :], pair_high) + dot_nt(gather[0:atoms, :], pair_low)
    centred = pair[:, 0:lane]
    for k in range(1, slots):
        centred = centred + pair[:, k * lane : (k + 1) * lane]
    arrive(sent3)
    in3_high, in3_low = split(in3[...])
    mine = mine + (dot(picked, in3_high) + dot(picked, in3_low))
    force_out[0, 0] = (centred - mine.T[0:8])[0:3]
    for copies in (sent0, sent1, sent2, sent3):
        for copy in copies:
            copy.wait_send()


def solution(mesh):
    sizes = (mesh.shape["gx"], mesh.shape["gy"])

    def per_device(*args):
        positions, neighbours = args[0], args[2]
        atoms = positions.shape[3]
        slots = neighbours.shape[2]
        edges = slots * atoms
        kinds, channels = args[6].shape
        width = args[8].shape[2]
        ghosts = 4 * args[4].shape[3] + 4 * args[5].shape[3]
        wide = 4 * channels
        scratch = [
            pltpu.VMEM((16, lane), f32),
            pltpu.VMEM((atoms + ghosts, edges), bf16),
            pltpu.VMEM((ghosts, atoms), bf16),
            pltpu.VMEM((atoms, 2 * lane), bf16),
            pltpu.VMEM((2, 7, channels, channels), bf16),
            pltpu.VMEM((2, 7, channels, channels), bf16),
            pltpu.VMEM((2, wide, 3 * width), bf16),
            pltpu.VMEM((4 * width, wide), bf16),
            pltpu.VMEM((2 * channels, edges), f32),
            pltpu.VMEM((wide, edges), f32),
            pltpu.VMEM((channels, edges), f32),
            pltpu.VMEM((wide, edges), f32),
            pltpu.VMEM((8, edges), f32),
            pltpu.VMEM((wide, atoms), f32),
            pltpu.VMEM((wide, atoms), f32),
            pltpu.VMEM((wide, edges), bf16),
            pltpu.VMEM((wide, edges), bf16),
            pltpu.VMEM((wide, edges), bf16),
            pltpu.VMEM((wide, edges), bf16),
            pltpu.VMEM((24, edges), f32),
            pltpu.VMEM((2 * width, edges), f32),
            pltpu.VMEM((2, 3 * width, edges), bf16),
            pltpu.VMEM((channels, 4 * lane), f32),
            pltpu.VMEM((channels, atoms), f32),
            pltpu.VMEM((wide, atoms), f32),
            pltpu.VMEM((wide, 2 * lane), bf16),
            pltpu.VMEM((atoms, wide), f32),
        ]
        for columns in (lane, wide, wide, lane):
            scratch += [pltpu.VMEM((ghosts, columns), f32)] * 2
        scratch += [pltpu.SemaphoreType.DMA((4, 8)), pltpu.SemaphoreType.DMA((4, 8))]
        vmem = pl.BlockSpec(memory_space=pltpu.VMEM)
        specs = [vmem] * len(args)
        specs[7] = pl.BlockSpec(memory_space=pltpu.SMEM)

        def body(*refs):
            kernel(sizes, *refs)

        return pl.pallas_call(
            body,
            out_shape=(
                jax.ShapeDtypeStruct((1, 1, atoms), f32),
                jax.ShapeDtypeStruct(positions.shape, f32),
            ),
            in_specs=specs,
            out_specs=(vmem, vmem),
            scratch_shapes=scratch,
            compiler_params=pltpu.CompilerParams(
                collective_id=0, has_side_effects=True, vmem_limit_bytes=48 * 1024 * 1024
            ),
        )(*args)

    return jax.shard_map(
        per_device,
        mesh=mesh,
        in_specs=(
            P(("rep", "gx"), "gy", None, None),
            P(("rep", "gx"), "gy", None),
            P(("rep", "gx"), "gy", None, None),
            P(("rep", "gx"), "gy", None),
            P(("rep", "gx"), "gy", None, None),
            P(("rep", "gx"), "gy", None, None),
            P(),
            P(),
            P(),
            P(),
            P(),
            P(),
            P(),
        ),
        out_specs=(P(("rep", "gx"), "gy", None), P(("rep", "gx"), "gy", None, None)),
        check_vma=False,
    )
```

profile of v0, /device:TPU:0, one launch (start us, length us, event | category | flops | bytes accessed | tf_op | source)
XLA Modules:
  0.0 45.5 jit_solution(11223037838352290363)
XLA Ops:
  0.6 0.0 copy-start.8
  0.6 0.0 copy-start.6
  0.7 0.0 copy-start.9
  0.7 0.7 %copy.15.refs_0_ = f32[1,1,3,128]{3,2,1,0:T(4,128)S(1)} copy(f32[1,1,3,128]{3,1,2,0:T(1,128)} %param.13) | data formatting | bytes 3072 | tf_op args[0]
  1.4 0.0 copy-done.8
  1.4 0.0 copy-done.6
  1.4 0.0 copy-done.9
  1.4 0.0 copy-start
  1.4 1.0 %copy-done = f32[2,3,128,128]{3,2,1,0:T(8,128)S(1)} copy-done((f32[2,3,128,128]{3,2,1,0:T(8,128)S(1)}, f32[2,3,128,128]{3,2,1,0:T(8,128)}, u32[]{:S(2)}) %copy-start) | copy-done | bytes 393240
  2.4 0.0 copy-start.1
  2.4 0.9 %copy-done.1 = f32[2,64,512]{2,1,0:T(8,128)S(1)} copy-done((f32[2,64,512]{2,1,0:T(8,128)S(1)}, f32[2,64,512]{2,1,0:T(8,128)}, u32[]{:S(2)}) %copy-start.1) | copy-done | bytes 262168
  3.3 0.0 copy-start.2
  3.3 0.8 %copy-done.2 = f32[128,128]{1,0:T(8,128)S(1)} copy-done((f32[128,128]{1,0:T(8,128)S(1)}, f32[128,128]{1,0:T(8,128)}, u32[]{:S(2)}) %copy-start.2) | copy-done | bytes 65560
  4.2 0.0 copy-start.3
  4.2 0.7 %copy-done.3 = f32[2,8,64]{2,1,0:T(8,128)S(1)} copy-done((f32[2,8,64]{2,1,0:T(8,128)S(1)}, f32[2,8,64]{2,1,0:T(8,128)}, u32[]{:S(2)}) %copy-start.3) | copy-done | bytes 4120
  4.9 0.0 copy-start.4
  4.9 0.7 %copy-done.4 = s32[1,1,8,128]{3,2,1,0:T(8,128)S(1)} copy-done((s32[1,1,8,128]{3,2,1,0:T(8,128)S(1)}, s32[1,1,8,128]{3,2,1,0:T(8,128)}, u32[]{:S(2)}) %copy-start.4) | copy-done | bytes 4120
  5.5 0.0 copy-start.5
  5.5 0.7 %copy-done.5 = f32[6,128]{1,0:T(8,128)S(1)} copy-done((f32[6,128]{1,0:T(8,128)S(1)}, f32[6,128]{1,0:T(8,128)}, u32[]{:S(2)}) %copy-start.5) | copy-done | bytes 3096
  6.2 0.0 copy-start.7
  6.2 0.7 %copy-done.7 = s32[1,1,4,8]{3,2,1,0:T(4,128)S(1)} copy-done((s32[1,1,4,8]{3,2,1,0:T(4,128)S(1)}, s32[1,1,4,8]{3,2,1,0:T(4,128)}, u32[]{:S(2)}) %copy-start.7) | copy-done | bytes 152
  6.9 0.0 copy-start.10
  6.9 0.7 %copy-done.10 = s32[1,1,128]{2,1,0:T(1,128)S(1)} copy-done((s32[1,1,128]{2,1,0:T(1,128)S(1)}, s32[1,1,128]{2,1,0:T(1,128)}, u32[]{:S(2)}) %copy-start.10) | copy-done | bytes 536
  7.6 0.0 copy-start.11
  7.6 0.7 %copy-done.11 = f32[6]{0:T(128)S(1)} copy-done((f32[6]{0:T(128)S(1)}, f32[6]{0:T(128)}, u32[]{:S(2)}) %copy-start.11) | copy-done | bytes 48
  8.2 36.2 %shard_map.140 = (f32[1,1,128]{2,1,0:T(1,128)S(1)}, f32[1,1,3,128]{3,2,1,0:T(4,128)S(1)}) custom-call(f32[1,1,3,128]{3,2,1,0:T(4,128)S(1)} %copy.15.refs_0_, s32[1,1,128]{2,1,0:T(1,128)S(1)} %copy-done.9, s32[1,1,8,128]{3,2,1,0:T(8,128)S(1)} %copy-done.4, s32[1,1,128]{2,1,0:T(1,128)S(1)} %copy-done.10, s32[1,1,4,32]{3,2,1,0:T(4,128)S(1)} %copy-done.6, ...), custom_call_target="tpu_custom_call" | custom-call | tf_op jit(solution)/shard_map/pallas_call | solution.py:536
  44.4 0.6 %copy.16 = f32[1,1,3,128]{3,1,2,0:T(1,128)} copy(f32[1,1,3,128]{3,2,1,0:T(4,128)S(1)} %get-tuple-element.3) | data formatting | bytes 3072 | tf_op jit(solution)/shard_map/pallas_call | solution.py:536
  45.0 0.5 %copy.18 = f32[1,1,128]{2,1,0:T(1,128)} copy(f32[1,1,128]{2,1,0:T(1,128)S(1)} %get-tuple-element.6) | data formatting | bytes 1024
Async XLA Ops:
  0.6 0.7 %copy-start.8 = (f32[2,128]{1,0:T(2,128)S(1)}, f32[2,128]{1,0:T(2,128)}, u32[]{:S(2)}) copy-start(f32[2,128]{1,0:T(2,128)} %refs_12_.1) | copy-start | bytes 3076
  0.6 0.7 %copy-start.6 = (s32[1,1,4,32]{3,2,1,0:T(4,128)S(1)}, s32[1,1,4,32]{3,2,1,0:T(4,128)}, u32[]{:S(2)}) copy-start(s32[1,1,4,32]{3,2,1,0:T(4,128)} %refs_4_.1) | copy-start | bytes 1540
  0.7 0.7 %copy-start.9 = (s32[1,1,128]{2,1,0:T(1,128)S(1)}, s32[1,1,128]{2,1,0:T(1,128)}, u32[]{:S(2)}) copy-start(s32[1,1,128]{2,1,0:T(1,128)} %refs_1_.1) | copy-start | bytes 1540
  1.4 1.0 %copy-start = (f32[2,3,128,128]{3,2,1,0:T(8,128)S(1)}, f32[2,3,128,128]{3,2,1,0:T(8,128)}, u32[]{:S(2)}) copy-start(f32[2,3,128,128]{3,2,1,0:T(8,128)} %refs_10_.1) | copy-start | bytes 1179652
  2.4 0.9 %copy-start.1 = (f32[2,64,512]{2,1,0:T(8,128)S(1)}, f32[2,64,512]{2,1,0:T(8,128)}, u32[]{:S(2)}) copy-start(f32[2,64,512]{2,1,0:T(8,128)} %refs_9_.1) | copy-start | bytes 786436
  3.3 0.8 %copy-start.2 = (f32[128,128]{1,0:T(8,128)S(1)}, f32[128,128]{1,0:T(8,128)}, u32[]{:S(2)}) copy-start(f32[128,128]{1,0:T(8,128)} %refs_11_.1) | copy-start | bytes 196612
  4.2 0.7 %copy-start.3 = (f32[2,8,64]{2,1,0:T(8,128)S(1)}, f32[2,8,64]{2,1,0:T(8,128)}, u32[]{:S(2)}) copy-start(f32[2,8,64]{2,1,0:T(8,128)} %refs_8_.1) | copy-start | bytes 12292
  4.9 0.7 %copy-start.4 = (s32[1,1,8,128]{3,2,1,0:T(8,128)S(1)}, s32[1,1,8,128]{3,2,1,0:T(8,128)}, u32[]{:S(2)}) copy-start(s32[1,1,8,128]{3,2,1,0:T(8,128)} %refs_2_.1) | copy-start | bytes 12292
  5.5 0.7 %copy-start.5 = (f32[6,128]{1,0:T(8,128)S(1)}, f32[6,128]{1,0:T(8,128)}, u32[]{:S(2)}) copy-start(f32[6,128]{1,0:T(8,128)} %refs_6_.1) | copy-start | bytes 9220
  6.2 0.7 %copy-start.7 = (s32[1,1,4,8]{3,2,1,0:T(4,128)S(1)}, s32[1,1,4,8]{3,2,1,0:T(4,128)}, u32[]{:S(2)}) copy-start(s32[1,1,4,8]{3,2,1,0:T(4,128)} %refs_5_.1) | copy-start | bytes 388
  6.9 0.7 %copy-start.10 = (s32[1,1,128]{2,1,0:T(1,128)S(1)}, s32[1,1,128]{2,1,0:T(1,128)}, u32[]{:S(2)}) copy-start(s32[1,1,128]{2,1,0:T(1,128)} %refs_3_.1) | copy-start | bytes 1540
  7.6 0.7 %copy-start.11 = (f32[6]{0:T(128)S(1)}, f32[6]{0:T(128)}, u32[]{:S(2)}) copy-start(f32[6]{0:T(128)} %refs_7_.1) | copy-start | bytes 76
where the time goes:
time: 45.9 us; the launch traced here: 45.5 us
  Pallas kernels  36.2 us (79%)
  local copies, waits for them, and re-layouts  8.63 us (19%)
  between operations  0.68 us (1%)
    pallas_call x1, Pallas kernels, per_device(): pl.pallas_call(body, out_shape=(jax.ShapeDtypeStruct((1, 1, atoms), f32),...  36.2 us
    unnamed x26, local copies, waits for them, and re-layouts  8.06 us

commit v1 on v0

--- a/solution.py
+++ b/solution.py
@@ -62,17 +62,22 @@
 
 def kernel(
     sizes,
+    *refs,
+):
+    inputs, energy_out, force_out, landed = refs[:13], refs[13], refs[14], refs[15:28]
+    (
     positions, species, neighbours, counts, faces, corners, embed, atom_energy,
     radial_in, radial_out, mixing, vector_mix, readout,
-    energy_out, force_out,
+    ) = landed
+    (
     small, gather, picks, picks_t, mix, mix_t, rad_t, rad, w1, w2, h1, h2, unit,
     message, grad_message, dw_high, dw_low, dh_high, dh_low, du, tangent, hidden,
     state, start, layer, features, back,
-    out0, in0, out1, in1, out2, in2, out3, in3, send_sem, recv_sem,
-):
+    out0, in0, out1, in1, out2, in2, out3, in3, send_sem, recv_sem, load_sem,
+    ) = refs[28:]
     count_x, count_y = sizes
     me_x, me_y = lax.axis_index("gx"), lax.axis_index("gy")
-    atoms = positions.shape[3]
+    atoms = neighbours.shape[3]
     slots = neighbours.shape[2]
     edges = slots * atoms
     kinds, channels = embed.shape
@@ -93,6 +98,13 @@
             "gy": lax.rem(me_y + sign * offset[1] + count_y, count_y),
         }
 
+    loads = [
+        pltpu.make_async_copy(inputs[m], landed[m], load_sem.at[m]) for m in range(len(inputs))
+    ]
+    first_loads = (4, 5, 0, 1)
+    later_loads = (2, 3, 9, 10, 11, 8, 6, 12, 7)
+    for m in first_loads + later_loads:
+        loads[m].start()
     barrier = pltpu.get_barrier_semaphore()
     for offset in offsets:
         pl.semaphore_signal(barrier, inc=1, device_id=place(offset, 1), device_id_type=MESH)
@@ -122,6 +134,8 @@
     def pad_rows(x, rows):
         return jnp.concatenate([x, jnp.zeros((rows - x.shape[0], x.shape[1]), x.dtype)], axis=0)
 
+    for m in first_loads:
+        loads[m].wait()
     chosen = jnp.concatenate(
         [faces[0, 0, f : f + 1, :] for f in range(4)]
         + [corners[0, 0, c : c + 1, :] for c in range(4)]
@@ -134,7 +148,7 @@
 
     code = species[0].astype(f32)
     small[...] = jnp.zeros_like(small)
-    small[0:3, :] = positions[0, 0]
+    small[0:3, :] = positions[0, :, 0, :]
     small[3:4, :] = code
     own = small[0:8, :]
     own_parts = thirds(own)
@@ -153,6 +167,8 @@
     out0[...] = packet + jnp.where(column == 0, shift_x, jnp.where(column == 1, shift_y, 0.0))
     pl.semaphore_wait(barrier, len(offsets))
     sent0 = exchange(0, out0, in0, -1)
+    for m in later_loads:
+        loads[m].wait()
 
     for k in range(slots):
         lanes = slice(k * lane, (k + 1) * lane)
@@ -476,7 +492,9 @@
     arrive(sent3)
     in3_high, in3_low = split(in3[...])
     mine = mine + (dot(picked, in3_high) + dot(picked, in3_low))
-    force_out[0, 0] = (centred - mine.T[0:8])[0:3]
+    force = centred - mine.T[0:8]
+    for m in range(3):
+        force_out[0, m] = force[m : m + 1, :]
     for copies in (sent0, sent1, sent2, sent3):
         for copy in copies:
             copy.wait_send()
@@ -486,15 +504,18 @@
     sizes = (mesh.shape["gx"], mesh.shape["gy"])
 
     def per_device(*args):
-        positions, neighbours = args[0], args[2]
-        atoms = positions.shape[3]
+        args = (jnp.transpose(args[0], (0, 2, 1, 3)),) + args[1:]
+        neighbours = args[2]
+        atoms = neighbours.shape[3]
         slots = neighbours.shape[2]
         edges = slots * atoms
         kinds, channels = args[6].shape
         width = args[8].shape[2]
         ghosts = 4 * args[4].shape[3] + 4 * args[5].shape[3]
         wide = 4 * channels
-        scratch = [
+        scratch = [pltpu.VMEM(a.shape, a.dtype) for a in args]
+        scratch[7] = pltpu.SMEM(args[7].shape, f32)
+        scratch += [
             pltpu.VMEM((16, lane), f32),
             pltpu.VMEM((atoms + ghosts, edges), bf16),
             pltpu.VMEM((ghosts, atoms), bf16),
@@ -526,26 +547,27 @@
         for columns in (lane, wide, wide, lane):
             scratch += [pltpu.VMEM((ghosts, columns), f32)] * 2
         scratch += [pltpu.SemaphoreType.DMA((4, 8)), pltpu.SemaphoreType.DMA((4, 8))]
+        scratch += [pltpu.SemaphoreType.DMA((len(args),))]
         vmem = pl.BlockSpec(memory_space=pltpu.VMEM)
-        specs = [vmem] * len(args)
-        specs[7] = pl.BlockSpec(memory_space=pltpu.SMEM)
+        specs = [pl.BlockSpec(memory_space=pltpu.MemorySpace.HBM)] * len(args)
 
         def body(*refs):
             kernel(sizes, *refs)
 
-        return pl.pallas_call(
+        energy, force = pl.pallas_call(
             body,
             out_shape=(
                 jax.ShapeDtypeStruct((1, 1, atoms), f32),
-                jax.ShapeDtypeStruct(positions.shape, f32),
+                jax.ShapeDtypeStruct(args[0].shape, f32),
             ),
             in_specs=specs,
             out_specs=(vmem, vmem),
             scratch_shapes=scratch,
             compiler_params=pltpu.CompilerParams(
-                collective_id=0, has_side_effects=True, vmem_limit_bytes=48 * 1024 * 1024
+                collective_id=0, has_side_effects=True, vmem_limit_bytes=64 * 1024 * 1024
             ),
         )(*args)
+        return energy, jnp.transpose(force, (0, 2, 1, 3))
 
     return jax.shard_map(
         per_device,

time: 45.9 us -> 39 us (0.85)
  local copies, waits for them, and re-layouts: 8.63 us -> 1.69 us
    unnamed x26 -> x6, local copies, waits for them, and re-layouts: 8.06 us -> 1.69 us
    pallas_call x1 -> x0, local copies, waits for them, and re-layouts: 0.56 us -> none  [per_device(): pl.pallas_call(body, out_shape=(jax.ShapeDtypeStruct((1, 1, atoms), f32),...]
where the time goes in v1:
time: 39 us; the launch traced here: 38.8 us
  Pallas kernels  36.4 us (93%)
  local copies, waits for them, and re-layouts  1.69 us (4%)
  between operations  0.66 us (2%)
    pallas_call x1, Pallas kernels, per_device(): pl.pallas_call(body, out_shape=(jax.ShapeDtypeStruct((1, 1, atoms), f32),...  36.4 us
    unnamed x6, local copies, waits for them, and re-layouts  1.69 us

profile of v1, /device:TPU:0, one launch (start us, length us, event | category | flops | bytes accessed | tf_op | source)
XLA Modules:
  0.0 38.8 jit_solution(7874060531528371165)
XLA Ops:
  0.6 36.4 %shard_map.140 = (f32[1,1,128]{2,1,0:T(1,128)}, f32[1,3,1,128]{3,2,1,0:T(1,128)}) custom-call(f32[1,3,1,128]{3,2,1,0:T(1,128)} %bitcast.5, s32[1,1,128]{2,1,0:T(1,128)} %refs_1_.1, s32[1,1,8,128]{3,2,1,0:T(8,128)} %refs_2_.1, s32[1,1,128]{2,1,0:T(1,128)} %refs_3_.1, s32[1,1,4,32]{3,2,1,0:T(4,128)} %refs_4_.1, s32[1,1,4,8]{3,2,1,0:T(4,128)} %refs_5_.1, ...), custom_call_target="tpu_custom_call" | custom-call | tf_op jit(solution)/shard_map/pallas_call | solution.py:557
  37.1 0.0 copy-start.1
  37.1 0.0 copy-start
  37.1 0.6 %copy-done.1 = f32[1,1,128]{2,1,0:T(1,128)S(1)} copy-done((f32[1,1,128]{2,1,0:T(1,128)S(1)}, f32[1,1,128]{2,1,0:T(1,128)}, u32[]{:S(2)}) %copy-start.1) | copy-done | bytes 536
  37.7 0.5 %copy.18 = f32[1,1,128]{2,1,0:T(1,128)} copy(f32[1,1,128]{2,1,0:T(1,128)S(1)} %copy-done.1) | data formatting | bytes 1024
  38.2 0.0 copy-done
  38.2 0.6 %copy.19 = f32[1,1,3,128]{3,1,2,0:T(1,128)} copy(f32[1,1,3,128]{3,1,2,0:T(1,128)S(1)} %bitcast.4) | data formatting | bytes 3072
Async XLA Ops:
  37.1 0.6 %copy-start.1 = (f32[1,1,128]{2,1,0:T(1,128)S(1)}, f32[1,1,128]{2,1,0:T(1,128)}, u32[]{:S(2)}) copy-start(f32[1,1,128]{2,1,0:T(1,128)} %get-tuple-element.10) | copy-start | bytes 1540
  37.1 1.1 %copy-start = (f32[1,3,1,128]{3,2,1,0:T(1,128)S(1)}, f32[1,3,1,128]{3,2,1,0:T(1,128)}, u32[]{:S(2)}) copy-start(f32[1,3,1,128]{3,2,1,0:T(1,128)} %get-tuple-element.5) | copy-start | bytes 4612
